TPU v7x, 32 devices: a whole 2x2x4 slice. The times are simulated.
32 devices in a mesh: fsdp: 4 (over y, x), dp: 8 (over z, core).
Axes of the slice: x: 2, y: 2, z: 4, core: 2. Of those that a mesh axis runs over, the one named last changes fastest.
Arguments:
- tokens: bfloat16 [4096, 4096], P(('fsdp', 'dp')), may hold values from -6 to 6
- master_old: float32 [480, 128, 128], P(('fsdp', 'dp')), may hold values from -0.25 to 0.25
- moment_old: float32 [480, 128, 128], P(('fsdp', 'dp')), may hold values from -6 to 6
- second_old: float32 [480, 128, 128], P(('fsdp', 'dp')), may hold values from 0.01 to 1
- old_cell: int32 [112, 4], P('fsdp'), may hold values from 0 to 119, as said below
- new_cell: int32 [112, 4], P('fsdp'), may hold values from 0 to 119, as said below
- regrown: int32 [112, 4], P('fsdp'), may hold values 0 or 1
- new_rows: int32 [112, 4], replicated, may hold values from 0 to 31, as said below
Outputs:
- hidden: bfloat16 [4096, 14336], P(('fsdp', 'dp'))
- master_new: float32 [480, 128, 128], P(('fsdp', 'dp'))
- moment_new: float32 [480, 128, 128], P(('fsdp', 'dp'))
- second_new: float32 [480, 128, 128], P(('fsdp', 'dp'))
Inputs may be any that keep to these rules, and one draw needn't show every extreme that they name: `old_cell`: within one fsdp index, taking its slots column by column and then by k, the old cells strictly increase; a cell's index // 15 is its holder along dp and index % 15 its place in that holder's buffer. `new_cell`: strictly increasing in the same order; every slot's new cell differs from its old cell by at most 8, and by exactly 8 for some slot of every fsdp index. `new_rows`: the 4 block rows of one block column are distinct.
All inputs are finite; a program needn't handle non-finite values. No bound on the sum of `regrown` on one device may be relied on, other than what follows from the above.
Results may differ from a plain program's by a relative error of at most 0.007.
Values may be sent and summed in bfloat16 or wider, within the bound.
A program may use at most 128 MiB of HBM per device.

v0:
```python
import jax
import jax.numpy as jnp
from jax import lax
from jax.sharding import PartitionSpec as P


def passed_along(block, axis, distance):
    devices = range(lax.axis_size(axis))
    route = [(i - distance, i) for i in devices if i - distance in devices]
    return lax.ppermute(block, axis, route)


def on_device(tokens, master_old, moment_old, second_old, old_cell, new_cell, regrown, new_rows):
    block_size = master_old.shape[1]
    capacity = master_old.shape[0]
    column_count = old_cell.shape[0]
    nonzero_count = old_cell.shape[1]
    slot_count = column_count * nonzero_count
    axis_width = lax.axis_size("dp")
    cell_count = axis_width * capacity
    farthest = min((cell_count - slot_count + capacity - 1) // capacity, axis_width - 1)
    holder = lax.axis_index("dp")
    old_flat = old_cell.reshape(-1)
    new_flat = new_cell.reshape(-1)
    keep_flag = regrown.reshape(-1) == 0
    my_cells = holder * capacity + jnp.arange(capacity, dtype=jnp.int32)
    matches = new_flat[None, :] == my_cells[:, None]
    present = jnp.any(matches & keep_flag[None, :], axis=1)
    source = jnp.sum(jnp.where(matches, old_flat[None, :], 0), axis=1)
    offset = holder - source // capacity
    slot_place = source % capacity
    candidate = jnp.where(offset > 0, 2 * offset - 1, jnp.where(offset < 0, -2 * offset, 0))
    pick_index = candidate * capacity + slot_place
    own_states = (master_old, moment_old, second_old)
    shift_list = []
    for distance in range(1, farthest + 1):
        shift_list.append(distance)
        shift_list.append(-distance)
    received_list = [own_states]
    for by_value in shift_list:
        received_list.append(
            (
                passed_along(own_states[0].astype(jnp.bfloat16), "dp", by_value).astype(
                    jnp.float32
                ),
                passed_along(own_states[1].astype(jnp.bfloat16), "dp", by_value).astype(
                    jnp.float32
                ),
                passed_along(own_states[2].astype(jnp.bfloat16), "dp", by_value).astype(
                    jnp.float32
                ),
            )
        )

    def settle(member):
        pool = jnp.concatenate([entry[member] for entry in received_list], axis=0)
        chosen = jnp.take(pool, pick_index, axis=0, mode="clip")
        return jnp.where(present[:, None, None], chosen, jnp.float32(0.0))

    master_new = settle(0)
    moment_new = settle(1)
    second_new = settle(2)
    cell_blocks = master_new.astype(jnp.bfloat16)
    group_cells = lax.all_gather(cell_blocks, "dp", axis=0, tiled=True)
    panel = jnp.take(group_cells, new_flat, axis=0).reshape(
        column_count, nonzero_count, block_size, block_size
    )
    token_count = tokens.shape[0]
    token_blocks = tokens.reshape(token_count, tokens.shape[1] // block_size, block_size)
    panel_piece = lax.all_gather(panel, "fsdp", axis=0, tiled=True)
    count = panel_piece.shape[0]
    picked = jnp.take(token_blocks, new_rows.reshape(-1), axis=1)
    picked = picked.reshape(token_count, count, nonzero_count, block_size)
    product = jnp.einsum("tcka,ckab->tcb", picked, panel_piece, preferred_element_type=jnp.float32)
    hidden = product.reshape(token_count, count * block_size).astype(jnp.bfloat16)
    return (hidden, master_new, moment_new, second_new)


def solution(mesh):
    return jax.shard_map(
        on_device,
        mesh=mesh,
        in_specs=(
            P(("fsdp", "dp"), None),
            P(("fsdp", "dp"), None, None),
            P(("fsdp", "dp"), None, None),
            P(("fsdp", "dp"), None, None),
            P("fsdp", None),
            P("fsdp", None),
            P("fsdp", None),
            P(),
        ),
        out_specs=(
            P(("fsdp", "dp"), None),
            P(("fsdp", "dp"), None, None),
            P(("fsdp", "dp"), None, None),
            P(("fsdp", "dp"), None, None),
        ),
        check_vma=False,
    )
```

profile of v0, /device:TPU:0, one launch (start us, length us, event | category | flops | bytes accessed | tf_op | source)
XLA Modules:
  0.0 267.9 jit_solution(17548049348519991265)
XLA Ops:
  7.2 0.0 all-gather.3.cloned.1.call-start
  7.2 1.3 convert_element_type.49
  8.5 1.3 collective-permute-start.3
  9.8 3.8 %collective-permute-start.2 = (bf16[15,128,128]{2,1,0:T(8,128)(2,1)S(1)}, bf16[15,128,128]{2,1,0:T(8,128)(2,1)}, u32[]{:S(2)}, u32[]{:S(2)}) collective-permute-start(bf16[15,128,128]{2,1,0:T(8,128)(2,1)S(1)} %convert_element_type.49), channel_id=1, source_target_pairs={{0,1},{1,2},{2,3},{3,4},{4,5},{5,6},{6,7},{8,9},{9,10},{10,11},{11... | collective-permute-start | bytes 1474568 | tf_op jit(solution)/shard_map/ppermute | solution.py:10
  13.6 1.3 convert_element_type.42
  14.9 1.3 collective-permute-start.1
  16.2 4.4 %collective-permute-start = (bf16[15,128,128]{2,1,0:T(8,128)(2,1)S(1)}, bf16[15,128,128]{2,1,0:T(8,128)(2,1)S(1)}, u32[]{:S(2)}, u32[]{:S(2)}) collective-permute-start(bf16[15,128,128]{2,1,0:T(8,128)(2,1)S(1)} %convert_element_type.42), channel_id=1, source_target_pairs={{0,1},{1,2},{2,3},{3,4},{4,5},{5,6},{6,7},{8,9},{9,10},{10,11},{11... | collective-permute-start | bytes 1474568 | tf_op jit(solution)/shard_map/ppermute | solution.py:10
  20.7 2.1 convert_element_type.52
  22.8 1.3 collective-permute-start.5
  24.1 0.1 copy.53
  24.2 0.1 reshape.187
  24.3 0.1 copy.55
  24.4 0.1 broadcast_in_dim.67
  24.5 0.2 fusion.6
  24.7 5.0 %collective-permute-start.4 = (bf16[15,128,128]{2,1,0:T(8,128)(2,1)}, bf16[15,128,128]{2,1,0:T(8,128)(2,1)}, u32[]{:S(2)}, u32[]{:S(2)}) collective-permute-start(bf16[15,128,128]{2,1,0:T(8,128)(2,1)} %convert_element_type.52), channel_id=1, source_target_pairs={{0,1},{1,2},{2,3},{3,4},{4,5},{5,6},{6,7},{8,9},{9,10},{10,11},{11... | collective-permute-start | bytes 1474568 | tf_op jit(solution)/shard_map/ppermute | solution.py:10
  29.8 0.1 copy.54
  29.9 0.1 eq.30
  30.0 0.2 fusion.7
  30.2 0.1 convert_element_type.44
  30.3 0.1 convert_element_type.43
  30.4 1.4 pad_maximum_fusion
  31.8 1.6 gather_fusion
  33.3 1.1 convert_element_type.51
  34.5 1.1 convert_element_type.50
  35.6 1.4 pad_maximum_fusion.1
  37.0 1.6 gather_fusion.3
  38.6 1.1 convert_element_type.54
  39.7 1.1 convert_element_type.53
  40.8 1.4 pad_maximum_fusion.2
  42.2 1.6 gather_fusion.4
  43.8 3.7 %broadcast_select_fusion.1 = (f32[15,128,128]{2,1,0:T(8,128)}, f32[15,128,128]{2,1,0:T(8,128)}, bf16[15,128,128]{2,1,0:T(8,128)(2,1)}, f32[15,128,128]{2,1,0:T(8,128)}) fusion(f32[15,128,128]{2,1,0:T(8,128)} %gather_fusion.4, pred[15]{0:T(512)(128)(4,1)S(1)} %fusion.7, f32[15,128,128]{2,1,0:T(8,128)} %gather_fusion.3, f32[15,128,128]{2,1,0:T(8,128)} %gather_fusion), kind=kLoop, calls=%fused_computation.14 | loop fusion | flops 983040 | bytes 6389775 | tf_op jit(solution)/shard_map/jit(_where)/select_n | solution.py:58
  47.5 0.0 all-gather.5.cloned.1.call-start
  47.6 0.1 reshape.188
  47.7 0.1 copy.52
  47.8 45.5 %all-gather.3.cloned.1.call-done = bf16[120,128,128]{2,1,0:T(8,128)(2,1)} async-done(((bf16[15,128,128]{2,1,0:T(8,128)(2,1)}), bf16[120,128,128]{2,1,0:T(8,128)(2,1)}) %all-gather.3.cloned.1.call-update) | async-done | bytes 3932176 | tf_op jit(solution)/shard_map/all_gather | solution.py:64
  93.3 5.0 %gather_fusion.1 = bf16[112,128,128]{2,1,0:T(8,128)(2,1)} fusion(bf16[120,128,128]{2,1,0:T(8,128)(2,1)} %all-gather.3.cloned.1.call-done, s32[1024]{0:T(1024)S(1)} %pad_clamp_fusion.1), kind=kCustom, calls=%fused_computation.1 | custom fusion | bytes 7340480 | tf_op jit(solution)/shard_map/jit(_take)/gather | solution.py:65
  98.3 4.3 %broadcast_select_fusion = bf16[28,4,128,128]{3,2,1,0:T(8,128)(2,1)} fusion(bf16[28,4,128,128]{3,2,1,0:T(8,128)(2,1)} %bitcast.38, pred[28,4]{1,0:T(8,128)(4,1)S(1)} %copy.52), kind=kLoop, calls=%fused_computation.10 | loop fusion | flops 1835008 | bytes 7340144 | tf_op jit(solution)/shard_map/jit(_take)/select_n | solution.py:65
  102.6 0.7 copy-done.2
  103.3 0.1 copy.59
  103.4 0.1 copy.57
  103.5 0.1 reshape.190
  103.6 0.2 copy-done
  103.8 0.7 copy.58
  104.5 0.7 copy.60
  105.2 13.3 %gather_fusion.2 = bf16[448,128,128]{2,1,0:T(8,128)(2,1)} fusion(bf16[128,32,128]{2,0,1:T(8,128)(2,1)S(1)} %copy.60, s32[1024]{0:T(1024)S(1)} %pad_clamp_fusion), kind=kCustom, calls=%fused_computation.2 | custom fusion | bytes 29361920 | tf_op jit(solution)/shard_map/jit(_take)/gather | solution.py:72
  118.5 123.1 %all-gather.5.cloned.1.call-done = bf16[112,4,128,128]{3,2,1,0:T(8,128)(2,1)} async-done(((bf16[28,4,128,128]{3,2,1,0:T(8,128)(2,1)}), bf16[112,4,128,128]{3,2,1,0:T(8,128)(2,1)}) %all-gather.5.cloned.1.call-update) | async-done | bytes 14680080 | tf_op jit(solution)/shard_map/all_gather | solution.py:70
  241.6 13.5 %bitcast_convert_fusion = bf16[112,128,128]{2,1,0:T(8,128)(2,1)} fusion(bf16[112,4,128,128]{3,2,1,0:T(8,128)(2,1)} %all-gather.5.cloned.1.call-done, bf16[128,112,4,128]{3,0,2,1:T(8,128)(2,1)} %bitcast.39, pred[112,4]{1,0:T(8,128)(4,1)S(1)} %copy.57), kind=kOutput, calls=%fused_computation.8 | convolution fusion | flops 1888223232 | bytes 33030592 | tf_op jit(solution)/shard_map/tcka,ckab->tcb/dot_general | solution.py:74
  255.0 6.1 %copy.62 = bf16[128,14336]{1,0:T(8,128)(2,1)} copy(bf16[128,14336]{0,1:T(8,128)(2,1)} %bitcast.41) | data formatting | bytes 7340032
  (26 shorter events, 0.1 us)
Async XLA Ops:
  7.2 16.9 %copy-start.4 = (s32[28,4]{0,1:T(4,128)S(1)}, s32[28,4]{0,1:T(4,128)}, u32[]{:S(2)}) copy-start(s32[28,4]{0,1:T(4,128)} %param.14) | copy-start | bytes 1348
  7.2 16.9 %copy-start.1 = (s32[28,4]{0,1:T(4,128)S(1)}, s32[28,4]{0,1:T(4,128)}, u32[]{:S(2)}) copy-start(s32[28,4]{0,1:T(4,128)} %param.13) | copy-start | bytes 1348
  7.2 17.1 %copy-start.3 = (s32[28,4]{0,1:T(4,128)S(1)}, s32[28,4]{0,1:T(4,128)}, u32[]{:S(2)}) copy-start(s32[28,4]{0,1:T(4,128)} %param.12) | copy-start | bytes 1348
  7.2 86.1 %all-gather.3.cloned.1.call-start = ((), (), s32[]{:S(2)}) async-start(), calls=%async_computation | async-start | bytes 4423680 | tf_op jit(solution)/shard_map/all_gather | solution.py:64
  8.5 24.8 %collective-permute-start.3 = (bf16[15,128,128]{2,1,0:T(8,128)(2,1)S(1)}, bf16[15,128,128]{2,1,0:T(8,128)(2,1)}, u32[]{:S(2)}, u32[]{:S(2)}) collective-permute-start(bf16[15,128,128]{2,1,0:T(8,128)(2,1)S(1)} %convert_element_type.49), channel_id=1, source_target_pairs={{1,0},{2,1},{3,2},{4,3},{5,4},{6,5},{7,6},{9,8},{10,9},{11,10},{12... | collective-permute-start | bytes 1474568 | tf_op jit(solution)/shard_map/ppermute | solution.py:10
  9.8 24.6 %collective-permute-start.2 = (bf16[15,128,128]{2,1,0:T(8,128)(2,1)S(1)}, bf16[15,128,128]{2,1,0:T(8,128)(2,1)}, u32[]{:S(2)}, u32[]{:S(2)}) collective-permute-start(bf16[15,128,128]{2,1,0:T(8,128)(2,1)S(1)} %convert_element_type.49), channel_id=1, source_target_pairs={{0,1},{1,2},{2,3},{3,4},{4,5},{5,6},{6,7},{8,9},{9,10},{10,11},{11... | collective-permute-start | bytes 1474568 | tf_op jit(solution)/shard_map/ppermute | solution.py:10
  14.9 9.8 %collective-permute-start.1 = (bf16[15,128,128]{2,1,0:T(8,128)(2,1)S(1)}, bf16[15,128,128]{2,1,0:T(8,128)(2,1)S(1)}, u32[]{:S(2)}, u32[]{:S(2)}) collective-permute-start(bf16[15,128,128]{2,1,0:T(8,128)(2,1)S(1)} %convert_element_type.42), channel_id=1, source_target_pairs={{1,0},{2,1},{3,2},{4,3},{5,4},{6,5},{7,6},{9,8},{10,9},{11,10},{12... | collective-permute-start | bytes 1474568 | tf_op jit(solution)/shard_map/ppermute | solution.py:10
  16.2 14.0 %collective-permute-start = (bf16[15,128,128]{2,1,0:T(8,128)(2,1)S(1)}, bf16[15,128,128]{2,1,0:T(8,128)(2,1)S(1)}, u32[]{:S(2)}, u32[]{:S(2)}) collective-permute-start(bf16[15,128,128]{2,1,0:T(8,128)(2,1)S(1)} %convert_element_type.42), channel_id=1, source_target_pairs={{0,1},{1,2},{2,3},{3,4},{4,5},{5,6},{6,7},{8,9},{9,10},{10,11},{11... | collective-permute-start | bytes 1474568 | tf_op jit(solution)/shard_map/ppermute | solution.py:10
  22.8 15.8 %collective-permute-start.5 = (bf16[15,128,128]{2,1,0:T(8,128)(2,1)}, bf16[15,128,128]{2,1,0:T(8,128)(2,1)}, u32[]{:S(2)}, u32[]{:S(2)}) collective-permute-start(bf16[15,128,128]{2,1,0:T(8,128)(2,1)} %convert_element_type.52), channel_id=1, source_target_pairs={{1,0},{2,1},{3,2},{4,3},{5,4},{6,5},{7,6},{9,8},{10,9},{11,10},{12... | collective-permute-start | bytes 1474568 | tf_op jit(solution)/shard_map/ppermute | solution.py:10
  24.7 15.0 %collective-permute-start.4 = (bf16[15,128,128]{2,1,0:T(8,128)(2,1)}, bf16[15,128,128]{2,1,0:T(8,128)(2,1)}, u32[]{:S(2)}, u32[]{:S(2)}) collective-permute-start(bf16[15,128,128]{2,1,0:T(8,128)(2,1)} %convert_element_type.52), channel_id=1, source_target_pairs={{0,1},{1,2},{2,3},{3,4},{4,5},{5,6},{6,7},{8,9},{9,10},{10,11},{11... | collective-permute-start | bytes 1474568 | tf_op jit(solution)/shard_map/ppermute | solution.py:10
  47.5 194.1 %all-gather.5.cloned.1.call-start = ((), (), s32[]{:S(2)}) async-start(), calls=%async_computation.1 | async-start | bytes 18350080 | tf_op jit(solution)/shard_map/all_gather | solution.py:70
  102.6 0.7 copy-start.2
  102.6 1.2 copy-start
Sparse Core Ops, SparseCore 0:
  47.6 45.6 all-gather.2
  102.7 138.7 all-gather.4
where the time goes:
time: 269 us; the launch traced here: 268 us
  waiting for transfers between devices  169 us (63%)
  local copies, waits for them, and re-layouts  32.4 us (12%)
  other arithmetic  21.9 us (8%)
  starting transfers between devices  17.2 us (6%)
  between operations  14.3 us (5%)
  matrix products  13.5 us (5%)
    all_gather x1, waiting for transfers between devices, on_device(): panel_piece = lax.all_gather(panel, 'fsdp', axis=0, tiled=True)  123 us
    all_gather x1, waiting for transfers between devices, on_device(): group_cells = lax.all_gather(cell_blocks, 'dp', axis=0, tiled=True)  45.5 us
    ppermute x6, starting transfers between devices, passed_along(): return lax.ppermute(block, axis, route)  17.1 us
    dot_general x1, matrix products, on_device(): jnp.einsum('tcka,ckab->tcb', picked, panel_piece, preferred_element_type=...  13.5 us
    gather x1, local copies, waits for them, and re-layouts, on_device(): picked = jnp.take(token_blocks, new_rows.reshape(-1), axis=1)  13.3 us
    unnamed x15, local copies, waits for them, and re-layouts  7.9 us
  transfers between devices with their start and end apart: 8, of which 2 were waited for; matrix products, arithmetic and copies ran while one was open for 11% of the time, Pallas kernels for 0%

commit v1 on v0

v1 whole, which is shorter than its diff:
```python
import functools

import jax
import jax.numpy as jnp
from jax import lax
from jax.experimental import pallas as pl
from jax.experimental.pallas import tpu as pltpu
from jax.sharding import PartitionSpec as P

MESH = pl.DeviceIdType.MESH
PIECES = 3
X, Y, UP, DOWN, TWIN = range(5)


def passed_along(block, axis, distance):
    devices = range(lax.axis_size(axis))
    route = [(i - distance, i) for i in devices if i - distance in devices]
    return lax.ppermute(block, axis, route)


def sources(old_cell, new_cell, regrown, capacity):
    old_flat, new_flat = old_cell.reshape(-1), new_cell.reshape(-1)
    kept = jnp.where(regrown.reshape(-1) == 0, old_flat, -1)
    my_cells = lax.axis_index("dp") * capacity + jnp.arange(capacity, dtype=jnp.int32)
    matches = new_flat[None, :] == my_cells[:, None]
    return jnp.max(jnp.where(matches, kept[None, :], -1), axis=1)


def on_device_plain(tokens, master_old, moment_old, second_old, old_cell, new_cell, regrown, new_rows):
    capacity, block_size = master_old.shape[0], master_old.shape[1]
    column_count, nonzero_count = old_cell.shape
    width = lax.axis_size("dp")
    holes = width * capacity - column_count * nonzero_count
    farthest = min((holes + capacity - 1) // capacity, width - 1)
    holder = lax.axis_index("dp")
    source = sources(old_cell, new_cell, regrown, capacity)
    present = source >= 0
    source = jnp.maximum(source, 0)
    offset = holder - source // capacity
    candidate = jnp.where(offset > 0, 2 * offset - 1, jnp.where(offset < 0, -2 * offset, 0))
    pick_index = candidate * capacity + source % capacity
    shifts = [s for distance in range(1, farthest + 1) for s in (distance, -distance)]

    def settle(state):
        narrow = state.astype(jnp.bfloat16)
        pool = [state] + [passed_along(narrow, "dp", s).astype(jnp.float32) for s in shifts]
        chosen = jnp.take(jnp.concatenate(pool, axis=0), pick_index, axis=0, mode="clip")
        return jnp.where(present[:, None, None], chosen, jnp.float32(0.0))

    cells = lax.all_gather(master_old.astype(jnp.bfloat16), "dp", axis=0, tiled=True)
    panel = jnp.take(cells, old_cell.reshape(-1), axis=0)
    panel = jnp.where(regrown.reshape(-1)[:, None, None] == 0, panel, jnp.bfloat16(0))
    panel = panel.reshape(column_count, nonzero_count, block_size, block_size)
    panel = lax.all_gather(panel, "fsdp", axis=0, tiled=True)
    count, token_count = panel.shape[0], tokens.shape[0]
    token_blocks = tokens.reshape(token_count, tokens.shape[1] // block_size, block_size)
    picked = jnp.take(token_blocks, new_rows.reshape(-1), axis=1)
    picked = picked.reshape(token_count, count, nonzero_count, block_size)
    product = jnp.einsum("tcka,ckab->tcb", picked, panel, preferred_element_type=jnp.float32)
    hidden = product.reshape(token_count, count * block_size).astype(jnp.bfloat16)
    return hidden, settle(master_old), settle(moment_old), settle(second_old)


def arrival_order(levels):
    order = []
    for dz in range(1 - levels, levels):
        away = abs(dz)
        for piece in range(PIECES):
            if away:
                order.append((3 * (away - 1) + piece + 1, 0, dz, piece))
            for role in (1, 2):
                key = 1 + piece if not away else (5 + 2 * piece if away == 1 else 6 + 2 * away + piece)
                order.append((key + 0.1, role, dz, piece))
            if piece < 2:
                key = 5 if not away else 7 + 2 * away + piece
            else:
                key = 6 if not away else 7.5 + 2.5 * away
            order.append((key + 0.2, 3, dz, piece))
    return sorted(order)


def kernel(
    levels, holes, columns, nonzero,
    pack_ref, rows_ref, tokens_ref, master_ref, moment_ref, second_ref,
    hidden_ref, master_out, moment_out, second_out,
    own, side_x, side_y, corner, hid0, hid1, hid2, hid3,
    tok, tok_blocks, mas, mom, sec, mom_narrow, sec_narrow, mom_halo, sec_halo,
    new_mas, new_mom, new_sec, packs, plan,
    load_sem, store_sem, plan_sem, pack_send, pack_recv, halo_send, halo_recv, send_sem, recv_sem,
):
    f, h = lax.axis_index("fsdp"), lax.axis_index("dp")
    z, core = h // 2, lax.rem(h, 2)
    capacity, block = mas.shape[0], mas.shape[1]
    cells = 2 * levels * capacity
    cuts = [capacity * i // PIECES for i in range(PIECES + 1)]
    groups = (own, side_x, side_y, corner)
    hids = (hid0, hid1, hid2, hid3)

    loads = [
        pltpu.make_async_copy(src, dst, load_sem.at[i])
        for i, (src, dst) in enumerate(
            [(master_ref, mas), (moment_ref, mom), (second_ref, sec), (tokens_ref, tok)]
        )
    ]
    for copy in loads:
        copy.start()

    barrier = pltpu.get_barrier_semaphore()

    def at(role, level, which):
        return (jnp.bitwise_xor(f, role), level * 2 + which)

    def greet(device):
        pl.semaphore_signal(barrier, inc=1, device_id=device, device_id_type=MESH)

    up, down = z + 1 < levels, z > 0
    other = 1 - core
    crossing = jnp.where(core == 1, up, down)
    cross_level = jnp.where(core == 1, z + 1, z - 1)

    for group in groups:
        group[cells] = jnp.zeros((block, block), jnp.bfloat16)
    mom_halo[...] = jnp.zeros_like(mom_halo)
    sec_halo[...] = jnp.zeros_like(sec_halo)

    for role in (1, 2, 3):
        greet(at(role, z, core))
    greet(at(0, z, other))

    @pl.when(up)
    def _():
        greet(at(0, z + 1, core))

    @pl.when(down)
    def _():
        greet(at(0, z - 1, core))

    @pl.when(crossing)
    def _():
        greet(at(0, cross_level, other))

    loads[0].wait()
    for j in range(capacity):
        own[h * capacity + j] = mas[j].astype(jnp.bfloat16)
    pl.semaphore_wait(barrier, 4 + up.astype(jnp.int32) + down.astype(jnp.int32) + crossing.astype(jnp.int32))

    sent = []

    def piece_ref(role, level, which, piece):
        first = (level * 2 + which) * capacity + cuts[piece]
        return groups[role].at[pl.ds(first, cuts[piece + 1] - cuts[piece])]

    def when(condition, act):
        if condition is True:
            act()
        else:
            pl.when(condition)(act)

    def send(condition, way, role, level, piece):
        target = {
            X: lambda: at(1, z, core), Y: lambda: at(2, z, core),
            UP: lambda: at(0, z + 1, core), DOWN: lambda: at(0, z - 1, core),
            TWIN: lambda: at(0, z, other),
        }[way]()
        there = role ^ {X: 1, Y: 2}.get(way, 0)
        copy = pltpu.make_async_remote_copy(
            src_ref=piece_ref(role, level, core, piece),
            dst_ref=piece_ref(there, level, core, piece),
            send_sem=send_sem.at[way, role, piece, level],
            recv_sem=recv_sem.at[1 if way == TWIN else 0, there, piece, level],
            device_id=target,
            device_id_type=MESH,
        )
        when(condition, copy.start)
        sent.append((condition, copy))

    def await_piece(lane, role, level, which, piece):
        part = piece_ref(role, level, which, piece)
        pltpu.make_async_remote_copy(
            src_ref=part, dst_ref=part, send_sem=send_sem.at[0, 0, 0, 0],
            recv_sem=recv_sem.at[lane, role, piece, level],
            device_id=at(0, z, other), device_id_type=MESH,
        ).wait_recv()

    def both(a, b):
        if a is True:
            return b
        return jnp.logical_and(a, b)

    def handle(role, dz, piece):
        level = z + dz
        if dz == 0:
            here = True
        else:
            here = level < levels if dz > 0 else level >= 0
        if (role, dz) != (0, 0):
            when(here, lambda: await_piece(0, role, level, core, piece))
        even = lax.rem(level + 2 * levels, 2) == 0
        if role == 0 or (role == 3 and piece < 2):
            if dz >= 0:
                send(both(here, down), DOWN, role, level, piece)
            if dz <= 0:
                send(both(here, up), UP, role, level, piece)
        if role == 0:
            send(here, X, role, level, piece)
            send(here, Y, role, level, piece)
        if role == 2:
            if piece == 0 and dz == 0:
                send(here, X, role, level, piece)
            if piece == 2:
                send(both(here, even), X, role, level, piece)
        if role == 1:
            if piece == 1 and dz == 0:
                send(here, Y, role, level, piece)
            if piece == 2:
                send(both(here, jnp.logical_not(even)), Y, role, level, piece)
        send(here, TWIN, role, level, piece)

    def compute(role, first, last):
        group, hid = groups[role], hids[role]
        base = jnp.bitwise_xor(f, role) * columns

        def column(c, carry):
            left = [tok_blocks[rows_ref[base + c, k]] for k in range(nonzero)]
            right = [group[plan[role, 0, c * nonzero + k]] for k in range(nonzero)]
            total = jnp.dot(
                jnp.concatenate(left, axis=1), jnp.concatenate(right, axis=0),
                preferred_element_type=jnp.float32,
            )
            hid[:, pl.ds(pl.multiple_of(c * block, block), block)] = total.astype(jnp.bfloat16)
            return carry

        lax.fori_loop(first, last, column, 0)

    for piece in range(PIECES):
        handle(0, 0, piece)

    pack_copies = []
    for role in (1, 2, 3):
        copy = pltpu.make_async_remote_copy(
            src_ref=pack_ref, dst_ref=packs.at[role - 1],
            send_sem=pack_send.at[role - 1], recv_sem=pack_recv.at[role - 1],
            device_id=at(role, z, core), device_id_type=MESH,
        )
        copy.start()
        pack_copies.append(copy)
    own_plan = pltpu.make_async_copy(pack_ref, plan.at[0], plan_sem.at[0])
    own_plan.start()

    halo_copies = []
    loads[1].wait()
    loads[2].wait()
    for state, narrow in ((mom, mom_narrow), (sec, sec_narrow)):
        for j in range(capacity):
            narrow[j] = state[j].astype(jnp.bfloat16)
    right, left = h + 1 < 2 * levels, h > 0
    for i, (narrow, halo) in enumerate(((mom_narrow, mom_halo), (sec_narrow, sec_halo))):
        for side, condition, first, place, holder in (
            (0, right, capacity - holes, 0, h + 1), (1, left, 0, holes, h - 1),
        ):
            copy = pltpu.make_async_remote_copy(
                src_ref=narrow.at[pl.ds(first, holes)], dst_ref=halo.at[pl.ds(place, holes)],
                send_sem=halo_send.at[i, side], recv_sem=halo_recv.at[i, side],
                device_id=(f, holder), device_id_type=MESH,
            )
            when(condition, copy.start)
            comes = left if side == 0 else right
            halo_copies.append((condition, comes, copy))
    loads[3].wait()
    for r in range(tok_blocks.shape[0]):
        tok_blocks[r] = tok[:, r * block : (r + 1) * block]

    def prepare():
        own_plan.wait()
        plans = []
        for role in (1, 2, 3):
            pack_copies[role - 1].wait_recv()
            copy = pltpu.make_async_copy(packs.at[role - 1], plan.at[role], plan_sem.at[role])
            copy.start()
            plans.append(copy)
        for copy in plans:
            copy.wait()

    def finish(role):
        for level in range(levels):
            for piece in range(PIECES):
                await_piece(1, role, level, other, piece)

    stores = []

    def store(src, dst):
        copy = pltpu.make_async_copy(src, dst, store_sem.at[len(stores)])
        copy.start()
        stores.append(copy)

    def store_hidden(role):
        first = pl.multiple_of(jnp.bitwise_xor(f, role) * (columns * block), block)
        store(hids[role], hidden_ref.at[:, pl.ds(first, columns * block)])

    def migrate():
        for condition, comes, copy in halo_copies:
            when(comes, copy.wait_recv)
        low = h * capacity

        def settle(j, carry):
            source = plan[0, 1, j]
            present = source >= 0
            place = source - low
            local = jnp.logical_and(place >= 0, place < capacity)
            inside = jnp.clip(place, 0, capacity - 1)
            beside = jnp.where(place < 0, place + holes, place - capacity + holes)
            beside = jnp.clip(beside, 0, 2 * holes - 1)
            zero = jnp.zeros((block, block), jnp.float32)
            cell = jnp.clip(source, 0, cells - 1)
            for state, moved, index, target in (
                (mas, own, cell, new_mas), (mom, mom_halo, beside, new_mom), (sec, sec_halo, beside, new_sec),
            ):
                value = jnp.where(local, state[inside], moved[index].astype(jnp.float32))
                target[j] = jnp.where(present, value, zero)
            return carry

        lax.fori_loop(0, capacity, settle, 0)
        store(new_mas, master_out)
        store(new_mom, moment_out)
        store(new_sec, second_out)

    parts = [columns * i // 4 for i in range(5)]
    extra = {10: [prepare, functools.partial(finish, 0), migrate]}
    for i in range(4):
        extra.setdefault(11 + i, []).append(functools.partial(compute, 0, parts[i], parts[i + 1]))
    extra[14].append(functools.partial(store_hidden, 0))
    waiting = sorted(extra)
    for key, role, dz, piece in arrival_order(levels):
        while waiting and waiting[0] <= key:
            for act in extra[waiting.pop(0)]:
                act()
        handle(role, dz, piece)
    for slot in waiting:
        for act in extra[slot]:
            act()
    for role in (1, 2, 3):
        finish(role)
        compute(role, 0, columns)
        store_hidden(role)

    for condition, copy in sent:
        when(condition, copy.wait_send)
    for copy in pack_copies:
        copy.wait_send()
    for condition, comes, copy in halo_copies:
        when(condition, copy.wait_send)
    for copy in stores:
        copy.wait()


def on_device_kernel(tokens, master_old, moment_old, second_old, old_cell, new_cell, regrown, new_rows):
    capacity, block = master_old.shape[0], master_old.shape[1]
    columns, nonzero = old_cell.shape
    width, ways = lax.axis_size("dp"), lax.axis_size("fsdp")
    levels, cells, slots = width // 2, width * capacity, columns * nonzero
    holes = cells - slots
    listed = jnp.where(regrown == 0, old_cell, cells).reshape(1, -1)
    source = sources(old_cell, new_cell, regrown, capacity).reshape(1, -1)
    lanes = 128
    pack = jnp.concatenate(
        [
            jnp.pad(listed, ((0, 0), (0, lanes - slots))),
            jnp.pad(source, ((0, 6), (0, lanes - capacity))),
        ],
        axis=0,
    )
    token_count = tokens.shape[0]
    bf, f32 = jnp.bfloat16, jnp.float32
    any_space = pl.BlockSpec(memory_space=pl.ANY)
    state = pltpu.VMEM((capacity, block, block), f32)
    narrow = pltpu.VMEM((capacity, block, block), bf)
    halo = pltpu.VMEM((2 * holes, block, block), bf)
    out_state = jax.ShapeDtypeStruct(master_old.shape, f32)
    return pl.pallas_call(
        functools.partial(kernel, levels, holes, columns, nonzero),
        out_shape=(
            jax.ShapeDtypeStruct((token_count, ways * columns * block), bf), out_state, out_state, out_state,
        ),
        in_specs=[
            pl.BlockSpec(memory_space=pltpu.VMEM), pl.BlockSpec(memory_space=pltpu.SMEM),
            any_space, any_space, any_space, any_space,
        ],
        out_specs=(any_space,) * 4,
        scratch_shapes=[pltpu.VMEM((cells + 1, block, block), bf)] * 4
        + [pltpu.VMEM((token_count, columns * block), bf)] * 4
        + [
            pltpu.VMEM(tokens.shape, bf),
            pltpu.VMEM((tokens.shape[1] // block, token_count, block), bf),
            state, state, state, narrow, narrow, halo, halo, state, state, state,
            pltpu.VMEM((3, 8, lanes), jnp.int32),
            pltpu.SMEM((4, 8, lanes), jnp.int32),
            pltpu.SemaphoreType.DMA((4,)),
            pltpu.SemaphoreType.DMA((7,)),
            pltpu.SemaphoreType.DMA((4,)),
            pltpu.SemaphoreType.DMA((3,)),
            pltpu.SemaphoreType.DMA((3,)),
            pltpu.SemaphoreType.DMA((2, 2)),
            pltpu.SemaphoreType.DMA((2, 2)),
            pltpu.SemaphoreType.DMA((5, 4, PIECES, levels)),
            pltpu.SemaphoreType.DMA((2, 4, PIECES, levels)),
        ],
        compiler_params=pltpu.CompilerParams(
            collective_id=0, has_side_effects=True, vmem_limit_bytes=50 * 1024 * 1024
        ),
        cost_estimate=pl.CostEstimate(
            flops=2 * token_count * ways * slots * block * block,
            bytes_accessed=30 * 1024 * 1024, transcendentals=0,
        ),
    )(pack, new_rows, tokens, master_old, moment_old, second_old)


def takes_kernel(mesh, slots, capacity):
    ways, width = mesh.shape["fsdp"], mesh.shape["dp"]
    holes = width * capacity - slots
    return ways == 4 and width % 2 == 0 and PIECES <= capacity and 0 < holes <= capacity and slots <= 128


def solution(mesh):
    def on_device(*args):
        slots, capacity = args[4].size, args[1].shape[0]
        chosen = on_device_kernel if takes_kernel(mesh, slots, capacity) else on_device_plain
        return chosen(*args)

    return jax.shard_map(
        on_device,
        mesh=mesh,
        in_specs=(
            P(("fsdp", "dp"), None),
            P(("fsdp", "dp"), None, None),
            P(("fsdp", "dp"), None, None),
            P(("fsdp", "dp"), None, None),
            P("fsdp", None),
            P("fsdp", None),
            P("fsdp", None),
            P(),
        ),
        out_specs=(
            P(("fsdp", "dp"), None),
            P(("fsdp", "dp"), None, None),
            P(("fsdp", "dp"), None, None),
            P(("fsdp", "dp"), None, None),
        ),
        check_vma=False,
    )
```

time: 269 us -> 107 us (0.40)
  waiting for transfers between devices: 169 us -> 0 us
  Pallas kernels: 0 us -> 94.2 us
  local copies, waits for them, and re-layouts: 32.4 us -> 10.3 us
  other arithmetic: 21.9 us -> 1.59 us
  starting transfers between devices: 17.2 us -> 0 us
  between operations: 14.3 us -> 0.68 us
  matrix products: 13.5 us -> 0 us
    all_gather x2 -> x0, waiting for transfers between devices: 169 us -> none  [the longest x1 123 us: on_device(): panel_piece = lax.all_gather(panel, 'fsdp', axis=0, tiled=True)]
    pallas_call x0 -> x1, Pallas kernels: none -> 94.2 us  [on_device_kernel(): pl.pallas_call(functools.partial(kernel, levels, holes, columns, nonzero)...]
    gather x5 -> x0, local copies, waits for them, and re-layouts: 23 us -> none  [the longest x1 13.3 us: on_device(): picked = jnp.take(token_blocks, new_rows.reshape(-1), axis=1)]
    ppermute x6 -> x0, starting transfers between devices: 17.1 us -> none  [passed_along(): return lax.ppermute(block, axis, route)]
    dot_general x1 -> x0, matrix products: 13.5 us -> none  [on_device(): jnp.einsum('tcka,ckab->tcb', picked, panel_piece, preferred_element_type=...]
    convert_element_type x9 -> x0, other arithmetic: 9.3 us -> none  [the longest x2 2.24 us: on_device(): passed_along(own_states[1].astype(jnp.bfloat16), 'dp', by_value)]
    select_n x4 -> x2, other arithmetic: 7.97 us -> 1.39 us  [the longest x1 0.71 us: on_device_kernel(): listed = jnp.where(regrown == 0, old_cell, cells).reshape(1, -1)]
    concatenate x3 -> x1, other arithmetic: 4.18 us -> 0.01 us  [on_device_kernel(): jnp.concatenate([jnp.pad(listed, ((0, 0), (0, lanes - slots))), jnp.pad(s...]
  transfers between devices with their start and end apart: 8 -> 0, of which waited for: 2 -> 0; matrix products, arithmetic and copies ran while one was open for 11% -> 0% of each run, Pallas kernels for 0% -> 0%
where the time goes in v1:
time: 107 us
  Pallas kernels  94.2 us (88%)
  local copies, waits for them, and re-layouts  10.3 us (10%)
  other arithmetic  1.59 us (1%)
    pallas_call x1, Pallas kernels, on_device_kernel(): pl.pallas_call(functools.partial(kernel, levels, holes, columns, nonzero)...  94.2 us
    unnamed x8, local copies, waits for them, and re-layouts  9.79 us

profile of v1, /device:TPU:0, one launch (start us, length us, event | category | flops | bytes accessed | tf_op | source)
XLA Modules:
  0.0 106.7 jit_solution(12875732872572541783)
XLA Ops:
  0.6 0.7 broadcast_select_fusion.1
  1.4 0.7 broadcast_select_fusion
  2.0 0.1 copy.22
  2.1 0.1 select_n.21
  2.2 0.1 copy.20
  2.3 0.1 reshape.35
  2.4 0.8 copy.21
  3.2 0.1 eq.30
  3.3 0.2 select_reduce_fusion
  3.5 0.8 copy.23.rows_ref
  4.3 0.0 copy-start
  4.3 1.2 %copy-done = f32[15,128,128]{2,1,0:T(8,128)S(1)} copy-done((f32[15,128,128]{2,1,0:T(8,128)S(1)}, f32[15,128,128]{2,1,0:T(8,128)}, u32[]{:S(2)}) %copy-start) | copy-done | bytes 983064
  5.5 94.2 %shard_map.111 = (bf16[128,14336]{1,0:T(8,128)(2,1)}, f32[15,128,128]{2,1,0:T(8,128)S(1)}, f32[15,128,128]{2,1,0:T(8,128)S(1)}, f32[15,128,128]{2,1,0:T(8,128)S(1)}) custom-call(s32[8,128]{1,0:T(8,128)S(1)} %pad_add_fusion.pack_ref, s32[112,4]{1,0:T(8,128)S(1)} %copy.23.rows_ref, bf16[128,4096]{1,0:T(8,128)(2,1)} %tokens_ref.1, f32[15,128,128]{2,1,0:T(8,128)S(1)} %copy-done, ...), custom_call_target="tpu_custom_call" | custom-call | flops 1879048192 | bytes 31457280 | tf_op jit(solution)/shard_map/pallas_call | solution.py:379
  99.7 4.2 %copy.28 = bf16[128,14336]{1,0:T(8,128)(2,1)} copy(bf16[128,14336]{1,0:T(8,128)(2,1)} %get-tuple-element.10) | data formatting | bytes 7340032
  103.9 0.9 copy.29
  104.9 0.9 copy.30
  105.8 0.9 copy.31
  (2 shorter events, 0.0 us)
Async XLA Ops:
  4.3 1.2 %copy-start = (f32[15,128,128]{2,1,0:T(8,128)S(1)}, f32[15,128,128]{2,1,0:T(8,128)}, u32[]{:S(2)}) copy-start(f32[15,128,128]{2,1,0:T(8,128)} %master_ref.1) | copy-start | bytes 2949124

commit v2 on v1

--- a/solution.py
+++ b/solution.py
@@ -61,22 +61,58 @@
     return hidden, settle(master_old), settle(moment_old), settle(second_old)
 
 
+def onward(levels, z, role, dz, piece):
+    steps = []
+    if role == 0 or (role == 3 and piece < 2):
+        steps += [(DOWN, z - 1, role)] if dz >= 0 and z > 0 else []
+        steps += [(UP, z + 1, role)] if dz <= 0 and z < levels - 1 else []
+    if role == 0:
+        steps += [(X, z, 1), (Y, z, 2)]
+    even = (z + dz) % 2 == 0
+    if role == 2 and ((piece == 0 and dz == 0) or (piece == 2 and even)):
+        steps.append((X, z, 3))
+    if role == 1 and ((piece == 1 and dz == 0) or (piece == 2 and not even)):
+        steps.append((Y, z, 3))
+    return steps
+
+
 def arrival_order(levels):
-    order = []
-    for dz in range(1 - levels, levels):
-        away = abs(dz)
-        for piece in range(PIECES):
-            if away:
-                order.append((3 * (away - 1) + piece + 1, 0, dz, piece))
-            for role in (1, 2):
-                key = 1 + piece if not away else (5 + 2 * piece if away == 1 else 6 + 2 * away + piece)
-                order.append((key + 0.1, role, dz, piece))
-            if piece < 2:
-                key = 5 if not away else 7 + 2 * away + piece
-            else:
-                key = 6 if not away else 7.5 + 2.5 * away
-            order.append((key + 0.2, 3, dz, piece))
-    return sorted(order)
+    others = [dz for dz in range(1 - levels, levels)]
+    order = [(r, dz, p) for dz in sorted(others, key=abs) for p in range(PIECES) for r in range(4) if r or dz]
+    order.sort(key=lambda k: abs(k[1]) + (k[0] in (1, 2)) + 2 * (k[0] == 3))
+    best = None
+    for _ in range(12):
+        script = [(0, 0, p) for p in range(PIECES)] + order
+        arrived, free = {}, {}
+        clock, place = [0.0] * levels, [0] * levels
+        while True:
+            nexts = []
+            for z in range(levels):
+                while place[z] < len(script) and not 0 <= z + script[place[z]][1] < levels:
+                    place[z] += 1
+                if place[z] < len(script):
+                    role, dz, piece = script[place[z]]
+                    came = 0.0 if (role, dz) == (0, 0) else arrived.get((z, role, dz, piece))
+                    if came is not None:
+                        nexts.append((max(clock[z], came), z))
+            if not nexts:
+                break
+            now, z = min(nexts)
+            role, dz, piece = script[place[z]]
+            place[z] += 1
+            for way, there, role_there in onward(levels, z, role, dz, piece):
+                now += 0.15
+                free[z, way] = max(free.get((z, way), 0.0), now) + 3.3
+                arrived[there, role_there, z + dz - there, piece] = free[z, way] + 1.0
+            clock[z] = now + 0.15
+        if best is None or max(clock) < best[0]:
+            best = (max(clock), order)
+        mean = {}
+        for key in order:
+            came = [arrived[z, key[0], key[1], key[2]] for z in range(levels) if 0 <= z + key[1] < levels]
+            mean[key] = sum(came) / len(came)
+        order = sorted(order, key=lambda k: (mean[k], k))
+    return best[1]
 
 
 def kernel(
@@ -219,18 +255,14 @@
     def compute(role, first, last):
         group, hid = groups[role], hids[role]
         base = jnp.bitwise_xor(f, role) * columns
-
-        def column(c, carry):
-            left = [tok_blocks[rows_ref[base + c, k]] for k in range(nonzero)]
-            right = [group[plan[role, 0, c * nonzero + k]] for k in range(nonzero)]
+        for c in range(first, last):
+            left = [tok_blocks[rows_ref[k, base + c]] for k in range(nonzero)]
+            right = [group[plan[role, k, c]] for k in range(nonzero)]
             total = jnp.dot(
                 jnp.concatenate(left, axis=1), jnp.concatenate(right, axis=0),
                 preferred_element_type=jnp.float32,
             )
-            hid[:, pl.ds(pl.multiple_of(c * block, block), block)] = total.astype(jnp.bfloat16)
-            return carry
-
-        lax.fori_loop(first, last, column, 0)
+            hid[:, c * block : (c + 1) * block] = total.astype(jnp.bfloat16)
 
     for piece in range(PIECES):
         handle(0, 0, piece)
@@ -303,8 +335,14 @@
         low = h * capacity
 
         def settle(j, carry):
-            source = plan[0, 1, j]
-            present = source >= 0
+            source = jnp.int32(cells)
+            for d in range(holes + 1):
+                slot = low + j - d
+                inside = jnp.clip(slot, 0, columns * nonzero - 1)
+                c, k = inside // nonzero, lax.rem(inside, nonzero)
+                match = jnp.logical_and(slot == inside, plan[0, nonzero + k, c] == low + j)
+                source = jnp.where(match, plan[0, k, c], source)
+            present = source < cells
             place = source - low
             local = jnp.logical_and(place >= 0, place < capacity)
             inside = jnp.clip(place, 0, capacity - 1)
@@ -325,23 +363,24 @@
         store(new_sec, second_out)
 
     parts = [columns * i // 4 for i in range(5)]
-    extra = {10: [prepare, functools.partial(finish, 0), migrate]}
-    for i in range(4):
-        extra.setdefault(11 + i, []).append(functools.partial(compute, 0, parts[i], parts[i + 1]))
-    extra[14].append(functools.partial(store_hidden, 0))
-    waiting = sorted(extra)
-    for key, role, dz, piece in arrival_order(levels):
-        while waiting and waiting[0] <= key:
-            for act in extra[waiting.pop(0)]:
-                act()
-        handle(role, dz, piece)
-    for slot in waiting:
-        for act in extra[slot]:
-            act()
-    for role in (1, 2, 3):
-        finish(role)
-        compute(role, 0, columns)
-        store_hidden(role)
+    order = arrival_order(levels)
+    last = {role: max(i for i, key in enumerate(order) if key[0] == role) for role in range(4)}
+    todo = []
+    for i, key in enumerate(order):
+        handle(*key)
+        if todo:
+            todo.pop(0)()
+        for role in range(4):
+            if last[role] == i:
+                if role == 0:
+                    todo += [prepare]
+                todo += [functools.partial(finish, role)]
+                todo += [functools.partial(compute, role, parts[n], parts[n + 1]) for n in range(4)]
+                todo += [functools.partial(store_hidden, role)]
+                if role == 0:
+                    todo += [migrate]
+    for act in todo:
+        act()
 
     for condition, copy in sent:
         when(condition, copy.wait_send)
@@ -359,16 +398,10 @@
     width, ways = lax.axis_size("dp"), lax.axis_size("fsdp")
     levels, cells, slots = width // 2, width * capacity, columns * nonzero
     holes = cells - slots
-    listed = jnp.where(regrown == 0, old_cell, cells).reshape(1, -1)
-    source = sources(old_cell, new_cell, regrown, capacity).reshape(1, -1)
     lanes = 128
-    pack = jnp.concatenate(
-        [
-            jnp.pad(listed, ((0, 0), (0, lanes - slots))),
-            jnp.pad(source, ((0, 6), (0, lanes - capacity))),
-        ],
-        axis=0,
-    )
+    listed = jnp.where(regrown == 0, old_cell, cells).T
+    pack = jnp.concatenate([listed, new_cell.T], axis=0)
+    pack = jnp.pad(pack, ((0, 8 - 2 * nonzero), (0, lanes - columns)))
     token_count = tokens.shape[0]
     bf, f32 = jnp.bfloat16, jnp.float32
     any_space = pl.BlockSpec(memory_space=pl.ANY)
@@ -405,19 +438,19 @@
             pltpu.SemaphoreType.DMA((2, 4, PIECES, levels)),
         ],
         compiler_params=pltpu.CompilerParams(
-            collective_id=0, has_side_effects=True, vmem_limit_bytes=50 * 1024 * 1024
+            collective_id=0, has_side_effects=True, vmem_limit_bytes=60 * 1024 * 1024
         ),
         cost_estimate=pl.CostEstimate(
             flops=2 * token_count * ways * slots * block * block,
             bytes_accessed=30 * 1024 * 1024, transcendentals=0,
         ),
-    )(pack, new_rows, tokens, master_old, moment_old, second_old)
+    )(pack, new_rows.T, tokens, master_old, moment_old, second_old)
 
 
 def takes_kernel(mesh, slots, capacity):
     ways, width = mesh.shape["fsdp"], mesh.shape["dp"]
     holes = width * capacity - slots
-    return ways == 4 and width % 2 == 0 and PIECES <= capacity and 0 < holes <= capacity and slots <= 128
+    return ways == 4 and width % 2 == 0 and PIECES <= capacity and 0 < holes <= capacity and slots <= 512
 
 
 def solution(mesh):

time: 107 us -> 83.1 us (0.78)
  Pallas kernels: 94.2 us -> 72.8 us
  local copies, waits for them, and re-layouts: 10.3 us -> 7.78 us
    pallas_call x1, Pallas kernels: 94.2 us -> 72.8 us  [on_device_kernel(): pl.pallas_call(functools.partial(kernel, levels, holes, columns, nonzero)...]
    unnamed x8 -> x10, local copies, waits for them, and re-layouts: 9.79 us -> 7.18 us
    select_n x2 -> x0, other arithmetic: 1.39 us -> none  [the longest x1 0.71 us: on_device_kernel(): listed = jnp.where(regrown == 0, old_cell, cells).reshape(1, -1)]
where the time goes in v2:
time: 83.1 us; the launch traced here: 82.7 us
  Pallas kernels  72.8 us (88%)
  local copies, waits for them, and re-layouts  7.78 us (9%)
  other arithmetic  1.39 us (2%)
    pallas_call x1, Pallas kernels, on_device_kernel(): pl.pallas_call(functools.partial(kernel, levels, holes, columns, nonzero)...  72.8 us
    unnamed x10, local copies, waits for them, and re-layouts  7.18 us

profile of v2, /device:TPU:0, one launch (start us, length us, event | category | flops | bytes accessed | tf_op | source)
XLA Modules:
  0.0 82.7 jit_solution(11416586519105050485)
XLA Ops:
  0.6 0.7 select_bitcast_fusion
  1.3 0.7 pad_add_fusion
  2.0 0.6 pad.4.pack_ref
  2.6 72.8 %shard_map.111 = (bf16[128,14336]{1,0:T(8,128)(2,1)}, f32[15,128,128]{2,1,0:T(8,128)}, f32[15,128,128]{2,1,0:T(8,128)}, f32[15,128,128]{2,1,0:T(8,128)}) custom-call(s32[8,128]{1,0:T(8,128)} %pad.4.pack_ref, s32[4,112]{1,0:T(4,128)} %bitcast.5, bf16[128,4096]{1,0:T(8,128)(2,1)} %tokens_ref.1, f32[15,128,128]{2,1,0:T(8,128)} %master_ref.1, ...), custom_call_target="tpu_custom_call" | custom-call | flops 1879048192 | bytes 31457280 | tf_op jit(solution)/shard_map/pallas_call | solution.py:412
  75.5 0.0 copy-start.2
  75.5 0.0 copy-start.1
  75.5 4.3 %copy.16 = bf16[128,14336]{1,0:T(8,128)(2,1)} copy(bf16[128,14336]{1,0:T(8,128)(2,1)} %get-tuple-element.8) | data formatting | bytes 7340032
  79.8 0.0 copy-done.2
  79.8 0.0 copy-start
  79.8 0.9 %copy.17 = f32[15,128,128]{2,1,0:T(8,128)} copy(f32[15,128,128]{2,1,0:T(8,128)S(1)} %copy-done.2) | data formatting | bytes 1966080
  80.8 0.0 copy-done.1
  80.8 0.9 %copy.18 = f32[15,128,128]{2,1,0:T(8,128)} copy(f32[15,128,128]{2,1,0:T(8,128)S(1)} %copy-done.1) | data formatting | bytes 1966080
  81.7 0.0 copy-done
  81.7 0.9 %copy.19 = f32[15,128,128]{2,1,0:T(8,128)} copy(f32[15,128,128]{2,1,0:T(8,128)S(1)} %copy-done) | data formatting | bytes 1966080
Async XLA Ops:
  75.5 4.4 %copy-start.2 = (f32[15,128,128]{2,1,0:T(8,128)S(1)}, f32[15,128,128]{2,1,0:T(8,128)}, u32[]{:S(2)}) copy-start(f32[15,128,128]{2,1,0:T(8,128)} %get-tuple-element.9) | copy-start | bytes 2949124
  75.5 5.3 %copy-start.1 = (f32[15,128,128]{2,1,0:T(8,128)S(1)}, f32[15,128,128]{2,1,0:T(8,128)}, u32[]{:S(2)}) copy-start(f32[15,128,128]{2,1,0:T(8,128)} %get-tuple-element.10) | copy-start | bytes 2949124
  79.8 1.9 %copy-start = (f32[15,128,128]{2,1,0:T(8,128)S(1)}, f32[15,128,128]{2,1,0:T(8,128)}, u32[]{:S(2)}) copy-start(f32[15,128,128]{2,1,0:T(8,128)} %get-tuple-element.11) | copy-start | bytes 2949124

commit v3 on v2

--- a/solution.py
+++ b/solution.py
@@ -8,8 +8,10 @@
 from jax.sharding import PartitionSpec as P
 
 MESH = pl.DeviceIdType.MESH
-PIECES = 3
+PIECES = 4
 X, Y, UP, DOWN, TWIN = range(5)
+KERNEL_VMEM = 105 * 1024 * 1024 // 2
+LAST_VMEM = 24 * 1024 * 1024
 
 
 def passed_along(block, axis, distance):
@@ -69,15 +71,20 @@
     if role == 0:
         steps += [(X, z, 1), (Y, z, 2)]
     even = (z + dz) % 2 == 0
-    if role == 2 and ((piece == 0 and dz == 0) or (piece == 2 and even)):
+    if role == 2 and ((piece == 0 and dz == 0) or piece == (2 if even else 3)):
         steps.append((X, z, 3))
-    if role == 1 and ((piece == 1 and dz == 0) or (piece == 2 and not even)):
+    if role == 1 and ((piece == 1 and dz == 0) or piece == (3 if even else 2)):
         steps.append((Y, z, 3))
     return steps
 
 
-def arrival_order(levels):
+def cuts_of(capacity):
+    return [-(-capacity * i // PIECES) for i in range(PIECES + 1)]
+
+
+def arrival_order(levels, capacity):
     others = [dz for dz in range(1 - levels, levels)]
+    cuts = cuts_of(capacity)
     order = [(r, dz, p) for dz in sorted(others, key=abs) for p in range(PIECES) for r in range(4) if r or dz]
     order.sort(key=lambda k: abs(k[1]) + (k[0] in (1, 2)) + 2 * (k[0] == 3))
     best = None
@@ -102,7 +109,7 @@
             place[z] += 1
             for way, there, role_there in onward(levels, z, role, dz, piece):
                 now += 0.15
-                free[z, way] = max(free.get((z, way), 0.0), now) + 3.3
+                free[z, way] = max(free.get((z, way), 0.0), now) + 0.66 * (cuts[piece + 1] - cuts[piece])
                 arrived[there, role_there, z + dz - there, piece] = free[z, way] + 1.0
             clock[z] = now + 0.15
         if best is None or max(clock) < best[0]:
@@ -115,22 +122,67 @@
     return best[1]
 
 
+def multiply(tok_blocks, rows_ref, base, group, plan, at, hid, first, last, nonzero):
+    block = group.shape[1]
+    for c in range(first, last):
+        left = [tok_blocks[rows_ref[k, base + c]] for k in range(nonzero)]
+        right = [group[plan[(*at, k, c)]] for k in range(nonzero)]
+        total = jnp.dot(
+            jnp.concatenate(left, axis=1), jnp.concatenate(right, axis=0),
+            preferred_element_type=jnp.float32,
+        )
+        hid[:, c * block : (c + 1) * block] = total.astype(jnp.bfloat16)
+
+
+def last_kernel(
+    columns, nonzero,
+    corner, hid0, hid1, hid2, new_mas, new_mom, new_sec, tok_blocks, packs, rows_ref,
+    hidden_ref, master_out, moment_out, second_out,
+    hid3, plan, plan_sem, store_sem,
+):
+    f = lax.axis_index("fsdp")
+    block = corner.shape[1]
+    listing = pltpu.make_async_copy(packs.at[2], plan, plan_sem)
+    listing.start()
+    stores = []
+
+    def store(src, dst):
+        copy = pltpu.make_async_copy(src, dst, store_sem.at[len(stores)])
+        copy.start()
+        stores.append(copy)
+
+    def hidden_part(role, first, last):
+        start = pl.multiple_of((jnp.bitwise_xor(f, role) * columns + first) * block, block)
+        return hidden_ref.at[:, pl.ds(start, (last - first) * block)]
+
+    for role, hid in enumerate((hid0, hid1, hid2)):
+        store(hid, hidden_part(role, 0, columns))
+    store(new_mas, master_out)
+    store(new_mom, moment_out)
+    store(new_sec, second_out)
+    listing.wait()
+    parts = [columns * i // 4 for i in range(5)]
+    for first, last in zip(parts, parts[1:]):
+        multiply(tok_blocks, rows_ref, jnp.bitwise_xor(f, 3) * columns, corner, plan, (), hid3, first, last, nonzero)
+        store(hid3.at[:, pl.ds(first * block, (last - first) * block)], hidden_part(3, first, last))
+    for copy in stores:
+        copy.wait()
+
+
 def kernel(
     levels, holes, columns, nonzero,
     pack_ref, rows_ref, tokens_ref, master_ref, moment_ref, second_ref,
-    hidden_ref, master_out, moment_out, second_out,
-    own, side_x, side_y, corner, hid0, hid1, hid2, hid3,
-    tok, tok_blocks, mas, mom, sec, mom_narrow, sec_narrow, mom_halo, sec_halo,
-    new_mas, new_mom, new_sec, packs, plan,
-    load_sem, store_sem, plan_sem, pack_send, pack_recv, halo_send, halo_recv, send_sem, recv_sem,
+    corner, hid0, hid1, hid2, new_mas, new_mom, new_sec, tok_blocks, packs,
+    own, side_x, side_y, tok, mas, mom, sec, mom_narrow, sec_narrow, mom_halo, sec_halo, plan,
+    load_sem, plan_sem, pack_send, pack_recv, halo_send, halo_recv, send_sem, recv_sem,
 ):
     f, h = lax.axis_index("fsdp"), lax.axis_index("dp")
     z, core = h // 2, lax.rem(h, 2)
     capacity, block = mas.shape[0], mas.shape[1]
     cells = 2 * levels * capacity
-    cuts = [capacity * i // PIECES for i in range(PIECES + 1)]
+    cuts = cuts_of(capacity)
     groups = (own, side_x, side_y, corner)
-    hids = (hid0, hid1, hid2, hid3)
+    hids = (hid0, hid1, hid2)
 
     loads = [
         pltpu.make_async_copy(src, dst, load_sem.at[i])
@@ -243,26 +295,18 @@
         if role == 2:
             if piece == 0 and dz == 0:
                 send(here, X, role, level, piece)
-            if piece == 2:
-                send(both(here, even), X, role, level, piece)
+            if piece >= 2:
+                send(both(here, even if piece == 2 else jnp.logical_not(even)), X, role, level, piece)
         if role == 1:
             if piece == 1 and dz == 0:
                 send(here, Y, role, level, piece)
-            if piece == 2:
-                send(both(here, jnp.logical_not(even)), Y, role, level, piece)
+            if piece >= 2:
+                send(both(here, even if piece == 3 else jnp.logical_not(even)), Y, role, level, piece)
         send(here, TWIN, role, level, piece)
 
     def compute(role, first, last):
-        group, hid = groups[role], hids[role]
         base = jnp.bitwise_xor(f, role) * columns
-        for c in range(first, last):
-            left = [tok_blocks[rows_ref[k, base + c]] for k in range(nonzero)]
-            right = [group[plan[role, k, c]] for k in range(nonzero)]
-            total = jnp.dot(
-                jnp.concatenate(left, axis=1), jnp.concatenate(right, axis=0),
-                preferred_element_type=jnp.float32,
-            )
-            hid[:, c * block : (c + 1) * block] = total.astype(jnp.bfloat16)
+        multiply(tok_blocks, rows_ref, base, groups[role], plan, (role,), hids[role], first, last, nonzero)
 
     for piece in range(PIECES):
         handle(0, 0, piece)
@@ -280,11 +324,6 @@
     own_plan.start()
 
     halo_copies = []
-    loads[1].wait()
-    loads[2].wait()
-    for state, narrow in ((mom, mom_narrow), (sec, sec_narrow)):
-        for j in range(capacity):
-            narrow[j] = state[j].astype(jnp.bfloat16)
     right, left = h + 1 < 2 * levels, h > 0
     for i, (narrow, halo) in enumerate(((mom_narrow, mom_halo), (sec_narrow, sec_halo))):
         for side, condition, first, place, holder in (
@@ -295,9 +334,17 @@
                 send_sem=halo_send.at[i, side], recv_sem=halo_recv.at[i, side],
                 device_id=(f, holder), device_id_type=MESH,
             )
+            halo_copies.append((condition, left if side == 0 else right, copy))
+
+    def send_halo():
+        for condition, comes, copy in halo_copies:
             when(condition, copy.start)
-            comes = left if side == 0 else right
-            halo_copies.append((condition, comes, copy))
+
+    loads[1].wait()
+    loads[2].wait()
+    for state, narrow in ((mom, mom_narrow), (sec, sec_narrow)):
+        for j in range(capacity):
+            narrow[j] = state[j].astype(jnp.bfloat16)
     loads[3].wait()
     for r in range(tok_blocks.shape[0]):
         tok_blocks[r] = tok[:, r * block : (r + 1) * block]
@@ -317,17 +364,6 @@
         for level in range(levels):
             for piece in range(PIECES):
                 await_piece(1, role, level, other, piece)
-
-    stores = []
-
-    def store(src, dst):
-        copy = pltpu.make_async_copy(src, dst, store_sem.at[len(stores)])
-        copy.start()
-        stores.append(copy)
-
-    def store_hidden(role):
-        first = pl.multiple_of(jnp.bitwise_xor(f, role) * (columns * block), block)
-        store(hids[role], hidden_ref.at[:, pl.ds(first, columns * block)])
 
     def migrate():
         for condition, comes, copy in halo_copies:
@@ -358,29 +394,24 @@
             return carry
 
         lax.fori_loop(0, capacity, settle, 0)
-        store(new_mas, master_out)
-        store(new_mom, moment_out)
-        store(new_sec, second_out)
 
     parts = [columns * i // 4 for i in range(5)]
-    order = arrival_order(levels)
+    order = arrival_order(levels, capacity)
     last = {role: max(i for i, key in enumerate(order) if key[0] == role) for role in range(4)}
     todo = []
     for i, key in enumerate(order):
         handle(*key)
         if todo:
             todo.pop(0)()
-        for role in range(4):
+        for role in range(3):
             if last[role] == i:
-                if role == 0:
-                    todo += [prepare]
+                todo += [send_halo, prepare] if role == 0 else []
                 todo += [functools.partial(finish, role)]
                 todo += [functools.partial(compute, role, parts[n], parts[n + 1]) for n in range(4)]
-                todo += [functools.partial(store_hidden, role)]
-                if role == 0:
-                    todo += [migrate]
+                todo += [migrate] if role == 0 else []
     for act in todo:
         act()
+    finish(3)
 
     for condition, copy in sent:
         when(condition, copy.wait_send)
@@ -388,9 +419,6 @@
         copy.wait_send()
     for condition, comes, copy in halo_copies:
         when(condition, copy.wait_send)
-    for copy in stores:
-        copy.wait()
-
 
 def on_device_kernel(tokens, master_old, moment_old, second_old, old_cell, new_cell, regrown, new_rows):
     capacity, block = master_old.shape[0], master_old.shape[1]
@@ -403,32 +431,26 @@
     pack = jnp.concatenate([listed, new_cell.T], axis=0)
     pack = jnp.pad(pack, ((0, 8 - 2 * nonzero), (0, lanes - columns)))
     token_count = tokens.shape[0]
-    bf, f32 = jnp.bfloat16, jnp.float32
+    bf, f32, i32 = jnp.bfloat16, jnp.float32, jnp.int32
     any_space = pl.BlockSpec(memory_space=pl.ANY)
+    vmem, smem = pl.BlockSpec(memory_space=pltpu.VMEM), pl.BlockSpec(memory_space=pltpu.SMEM)
     state = pltpu.VMEM((capacity, block, block), f32)
     narrow = pltpu.VMEM((capacity, block, block), bf)
     halo = pltpu.VMEM((2 * holes, block, block), bf)
-    out_state = jax.ShapeDtypeStruct(master_old.shape, f32)
-    return pl.pallas_call(
+    group = pltpu.VMEM((cells + 1, block, block), bf)
+    hid = pltpu.VMEM((token_count, columns * block), bf)
+    tok_blocks = pltpu.VMEM((tokens.shape[1] // block, token_count, block), bf)
+    rows = new_rows.T
+    flops = 2 * token_count * slots * block * block
+    between = pl.pallas_call(
         functools.partial(kernel, levels, holes, columns, nonzero),
-        out_shape=(
-            jax.ShapeDtypeStruct((token_count, ways * columns * block), bf), out_state, out_state, out_state,
-        ),
-        in_specs=[
-            pl.BlockSpec(memory_space=pltpu.VMEM), pl.BlockSpec(memory_space=pltpu.SMEM),
-            any_space, any_space, any_space, any_space,
-        ],
-        out_specs=(any_space,) * 4,
-        scratch_shapes=[pltpu.VMEM((cells + 1, block, block), bf)] * 4
-        + [pltpu.VMEM((token_count, columns * block), bf)] * 4
-        + [
-            pltpu.VMEM(tokens.shape, bf),
-            pltpu.VMEM((tokens.shape[1] // block, token_count, block), bf),
-            state, state, state, narrow, narrow, halo, halo, state, state, state,
-            pltpu.VMEM((3, 8, lanes), jnp.int32),
-            pltpu.SMEM((4, 8, lanes), jnp.int32),
+        out_shape=(group, hid, hid, hid, state, state, state, tok_blocks, pltpu.VMEM((3, 8, lanes), i32)),
+        in_specs=[vmem, smem, any_space, any_space, any_space, any_space],
+        out_specs=(vmem,) * 9,
+        scratch_shapes=[
+            group, group, group, pltpu.VMEM(tokens.shape, bf), state, state, state, narrow, narrow, halo, halo,
+            pltpu.SMEM((4, 8, lanes), i32),
             pltpu.SemaphoreType.DMA((4,)),
-            pltpu.SemaphoreType.DMA((7,)),
             pltpu.SemaphoreType.DMA((4,)),
             pltpu.SemaphoreType.DMA((3,)),
             pltpu.SemaphoreType.DMA((3,)),
@@ -438,13 +460,29 @@
             pltpu.SemaphoreType.DMA((2, 4, PIECES, levels)),
         ],
         compiler_params=pltpu.CompilerParams(
-            collective_id=0, has_side_effects=True, vmem_limit_bytes=60 * 1024 * 1024
+            collective_id=0, has_side_effects=True, vmem_limit_bytes=KERNEL_VMEM
         ),
         cost_estimate=pl.CostEstimate(
-            flops=2 * token_count * ways * slots * block * block,
-            bytes_accessed=30 * 1024 * 1024, transcendentals=0,
+            flops=3 * flops, bytes_accessed=16 * 1024 * 1024, transcendentals=0
         ),
-    )(pack, new_rows.T, tokens, master_old, moment_old, second_old)
+    )(pack, rows, tokens, master_old, moment_old, second_old)
+    out_state = jax.ShapeDtypeStruct(master_old.shape, f32)
+    return pl.pallas_call(
+        functools.partial(last_kernel, columns, nonzero),
+        out_shape=(
+            jax.ShapeDtypeStruct((token_count, ways * columns * block), bf), out_state, out_state, out_state,
+        ),
+        in_specs=[vmem] * 9 + [smem],
+        out_specs=(any_space,) * 4,
+        scratch_shapes=[
+            hid,
+            pltpu.SMEM((8, lanes), i32),
+            pltpu.SemaphoreType.DMA,
+            pltpu.SemaphoreType.DMA((10,)),
+        ],
+        compiler_params=pltpu.CompilerParams(vmem_limit_bytes=LAST_VMEM),
+        cost_estimate=pl.CostEstimate(flops=flops, bytes_accessed=8 * 1024 * 1024, transcendentals=0),
+    )(*between, rows)
 
 
 def takes_kernel(mesh, slots, capacity):

time: 83.1 us -> 78.9 us (0.949)
  local copies, waits for them, and re-layouts: 7.78 us -> 0.6 us
  Pallas kernels: 72.8 us -> 75.9 us
    unnamed x10 -> x2, local copies, waits for them, and re-layouts: 7.18 us -> 0.01 us
    pallas_call x0 -> x1, Pallas kernels: none -> 3.42 us  [on_device_kernel(): pl.pallas_call(functools.partial(last_kernel, columns, nonzero), out_shap...]
where the time goes in v3:
time: 78.9 us; the launch traced here: 78.6 us
  Pallas kernels  75.9 us (96%)
  other arithmetic  1.4 us (2%)
    pallas_call x1, Pallas kernels, on_device_kernel(): pl.pallas_call(functools.partial(kernel, levels, holes, columns, nonzero)...  72.5 us
    pallas_call x1, Pallas kernels, on_device_kernel(): pl.pallas_call(functools.partial(last_kernel, columns, nonzero), out_shap...  3.42 us

profile of v3, /device:TPU:0, one launch (start us, length us, event | category | flops | bytes accessed | tf_op | source)
XLA Modules:
  0.0 78.6 jit_solution(2890930729360868930)
XLA Ops:
  0.6 0.0 copy-start
  0.6 0.7 select_bitcast_fusion
  1.3 0.7 pad_add_fusion
  2.0 0.6 pad.4.pack_ref
  2.6 72.5 %shard_map.111 = (bf16[121,128,128]{2,1,0:T(8,128)(2,1)S(1)}, bf16[128,3584]{1,0:T(8,128)(2,1)S(1)}, bf16[128,3584]{1,0:T(8,128)(2,1)S(1)}, bf16[128,3584]{1,0:T...) custom-call(s32[8,128]{1,0:T(8,128)} %pad.4.pack_ref, ...), custom_call_target="tpu_custom_call" | custom-call | flops 1409286144 | bytes 16777216 | tf_op jit(solution)/shard_map/pallas_call | solution.py:445
  75.1 0.0 copy-done
  75.2 3.4 %shard_map.112 = (bf16[128,14336]{1,0:T(8,128)(2,1)}, f32[15,128,128]{2,1,0:T(8,128)}, f32[15,128,128]{2,1,0:T(8,128)}, f32[15,128,128]{2,1,0:T(8,128)}) custom-call(bf16[121,128,128]{2,1,0:T(8,128)(2,1)S(1)} %get-tuple-element.13.corner, bf16[128,3584]{1,0:T(8,128)(2,1)S(1)} %get-tuple-element.14.hid0, bf16[128,3584]{1,0:T(8,128)(2,1)S(1)} %get-tuple-element.15.hid1, ...), custom_call_target="tpu_custom_call" | custom-call | flops 469762048 | bytes 8388608 | tf_op jit(solution)/shard_map/pallas_call | solution.py:470
Async XLA Ops:
  0.6 74.5 %copy-start = (s32[112,4]{0,1:T(4,128)S(1)}, s32[112,4]{0,1:T(4,128)}, u32[]{:S(2)}) copy-start(s32[112,4]{0,1:T(4,128)} %param.15) | copy-start | bytes 5380

commit v4 on v3

--- a/solution.py
+++ b/solution.py
@@ -88,7 +88,8 @@
     order = [(r, dz, p) for dz in sorted(others, key=abs) for p in range(PIECES) for r in range(4) if r or dz]
     order.sort(key=lambda k: abs(k[1]) + (k[0] in (1, 2)) + 2 * (k[0] == 3))
     best = None
-    for _ in range(12):
+    total = 0.66 * 5.2 * capacity
+    for turn in range(14):
         script = [(0, 0, p) for p in range(PIECES)] + order
         arrived, free = {}, {}
         clock, place = [0.0] * levels, [0] * levels
@@ -112,12 +113,17 @@
                 free[z, way] = max(free.get((z, way), 0.0), now) + 0.66 * (cuts[piece + 1] - cuts[piece])
                 arrived[there, role_there, z + dz - there, piece] = free[z, way] + 1.0
             clock[z] = now + 0.15
-        if best is None or max(clock) < best[0]:
+        if turn >= 2 and (best is None or max(clock) < best[0]):
             best = (max(clock), order)
         mean = {}
         for key in order:
             came = [arrived[z, key[0], key[1], key[2]] for z in range(levels) if 0 <= z + key[1] < levels]
-            mean[key] = sum(came) / len(came)
+            held = 0.0
+            if key[0] == 3:
+                held = 0.87 if key[2] >= 2 else 0.4
+            elif key[0] and key[2] >= 2:
+                held = 0.68
+            mean[key] = max(sum(came) / len(came), held * total)
         order = sorted(order, key=lambda k: (mean[k], k))
     return best[1]
 
@@ -408,9 +414,9 @@
                 todo += [send_halo, prepare] if role == 0 else []
                 todo += [functools.partial(finish, role)]
                 todo += [functools.partial(compute, role, parts[n], parts[n + 1]) for n in range(4)]
-                todo += [migrate] if role == 0 else []
     for act in todo:
         act()
+    migrate()
     finish(3)
 
     for condition, copy in sent:

time: 78.9 us -> 74.2 us (0.940)
  Pallas kernels: 75.9 us -> 71.3 us
    pallas_call x1, Pallas kernels: 72.5 us -> 67.9 us  [on_device_kernel(): pl.pallas_call(functools.partial(kernel, levels, holes, columns, nonzero)...]
where the time goes in v4:
time: 74.2 us; the launch traced here: 73.9 us
  Pallas kernels  71.3 us (96%)
  other arithmetic  1.4 us (2%)
    pallas_call x1, Pallas kernels, on_device_kernel(): pl.pallas_call(functools.partial(kernel, levels, holes, columns, nonzero)...  67.9 us
    pallas_call x1, Pallas kernels, on_device_kernel(): pl.pallas_call(functools.partial(last_kernel, columns, nonzero), out_shap...  3.42 us

profile of v4, /device:TPU:0, one launch (start us, length us, event | category | flops | bytes accessed | tf_op | source)
XLA Modules:
  0.0 73.9 jit_solution(14784954070794837857)
XLA Ops:
  0.6 0.0 copy-start
  0.6 0.7 select_bitcast_fusion
  1.3 0.7 pad_add_fusion
  2.0 0.6 pad.4.pack_ref
  2.6 67.9 %shard_map.111 = (bf16[121,128,128]{2,1,0:T(8,128)(2,1)S(1)}, bf16[128,3584]{1,0:T(8,128)(2,1)S(1)}, bf16[128,3584]{1,0:T(8,128)(2,1)S(1)}, bf16[128,3584]{1,0:T...) custom-call(s32[8,128]{1,0:T(8,128)} %pad.4.pack_ref, ...), custom_call_target="tpu_custom_call" | custom-call | flops 1409286144 | bytes 16777216 | tf_op jit(solution)/shard_map/pallas_call | solution.py:451
  70.5 0.0 copy-done
  70.5 3.4 %shard_map.112 = (bf16[128,14336]{1,0:T(8,128)(2,1)}, f32[15,128,128]{2,1,0:T(8,128)}, f32[15,128,128]{2,1,0:T(8,128)}, f32[15,128,128]{2,1,0:T(8,128)}) custom-call(bf16[121,128,128]{2,1,0:T(8,128)(2,1)S(1)} %get-tuple-element.13.corner, bf16[128,3584]{1,0:T(8,128)(2,1)S(1)} %get-tuple-element.14.hid0, bf16[128,3584]{1,0:T(8,128)(2,1)S(1)} %get-tuple-element.15.hid1, ...), custom_call_target="tpu_custom_call" | custom-call | flops 469762048 | bytes 8388608 | tf_op jit(solution)/shard_map/pallas_call | solution.py:476
Async XLA Ops:
  0.6 69.9 %copy-start = (s32[112,4]{0,1:T(4,128)S(1)}, s32[112,4]{0,1:T(4,128)}, u32[]{:S(2)}) copy-start(s32[112,4]{0,1:T(4,128)} %param.15) | copy-start | bytes 5380

commit v5 on v4

--- a/solution.py
+++ b/solution.py
@@ -142,14 +142,18 @@
 
 def last_kernel(
     columns, nonzero,
-    corner, hid0, hid1, hid2, new_mas, new_mom, new_sec, tok_blocks, packs, rows_ref,
+    corner, hid0, hid1, hid2, new_mas, new_mom, new_sec, tok_blocks, packs, rows_in,
     hidden_ref, master_out, moment_out, second_out,
-    hid3, plan, plan_sem, store_sem,
+    hid3, plan, rows_ref, plan_sem, store_sem,
 ):
     f = lax.axis_index("fsdp")
     block = corner.shape[1]
-    listing = pltpu.make_async_copy(packs.at[2], plan, plan_sem)
-    listing.start()
+    listings = [
+        pltpu.make_async_copy(packs.at[2], plan, plan_sem.at[0]),
+        pltpu.make_async_copy(rows_in, rows_ref, plan_sem.at[1]),
+    ]
+    for copy in listings:
+        copy.start()
     stores = []
 
     def store(src, dst):
@@ -166,7 +170,8 @@
     store(new_mas, master_out)
     store(new_mom, moment_out)
     store(new_sec, second_out)
-    listing.wait()
+    for copy in listings:
+        copy.wait()
     parts = [columns * i // 4 for i in range(5)]
     for first, last in zip(parts, parts[1:]):
         multiply(tok_blocks, rows_ref, jnp.bitwise_xor(f, 3) * columns, corner, plan, (), hid3, first, last, nonzero)
@@ -177,10 +182,10 @@
 
 def kernel(
     levels, holes, columns, nonzero,
-    pack_ref, rows_ref, tokens_ref, master_ref, moment_ref, second_ref,
+    old_in, new_in, regrown_in, rows_in, tokens_ref, master_ref, moment_ref, second_ref,
     corner, hid0, hid1, hid2, new_mas, new_mom, new_sec, tok_blocks, packs,
     own, side_x, side_y, tok, mas, mom, sec, mom_narrow, sec_narrow, mom_halo, sec_halo, plan,
-    load_sem, plan_sem, pack_send, pack_recv, halo_send, halo_recv, send_sem, recv_sem,
+    old_list, new_list, regrown_list, pack_ref, rows_ref, load_sem, plan_sem, pack_send, pack_recv, halo_send, halo_recv, send_sem, recv_sem,
 ):
     f, h = lax.axis_index("fsdp"), lax.axis_index("dp")
     z, core = h // 2, lax.rem(h, 2)
@@ -193,7 +198,10 @@
     loads = [
         pltpu.make_async_copy(src, dst, load_sem.at[i])
         for i, (src, dst) in enumerate(
-            [(master_ref, mas), (moment_ref, mom), (second_ref, sec), (tokens_ref, tok)]
+            [
+                (master_ref, mas), (moment_ref, mom), (second_ref, sec), (tokens_ref, tok),
+                (old_in, old_list), (new_in, new_list), (regrown_in, regrown_list), (rows_in, rows_ref),
+            ]
         )
     ]
     for copy in loads:
@@ -317,6 +325,11 @@
     for piece in range(PIECES):
         handle(0, 0, piece)
 
+    for copy in loads[4:]:
+        copy.wait()
+    pack_ref[...] = jnp.zeros_like(pack_ref)
+    pack_ref[:nonzero, :columns] = jnp.where(regrown_list[...] == 0, old_list[...], cells)
+    pack_ref[nonzero : 2 * nonzero, :columns] = new_list[...]
     pack_copies = []
     for role in (1, 2, 3):
         copy = pltpu.make_async_remote_copy(
@@ -433,13 +446,10 @@
     levels, cells, slots = width // 2, width * capacity, columns * nonzero
     holes = cells - slots
     lanes = 128
-    listed = jnp.where(regrown == 0, old_cell, cells).T
-    pack = jnp.concatenate([listed, new_cell.T], axis=0)
-    pack = jnp.pad(pack, ((0, 8 - 2 * nonzero), (0, lanes - columns)))
     token_count = tokens.shape[0]
     bf, f32, i32 = jnp.bfloat16, jnp.float32, jnp.int32
     any_space = pl.BlockSpec(memory_space=pl.ANY)
-    vmem, smem = pl.BlockSpec(memory_space=pltpu.VMEM), pl.BlockSpec(memory_space=pltpu.SMEM)
+    vmem = pl.BlockSpec(memory_space=pltpu.VMEM)
     state = pltpu.VMEM((capacity, block, block), f32)
     narrow = pltpu.VMEM((capacity, block, block), bf)
     halo = pltpu.VMEM((2 * holes, block, block), bf)
@@ -447,16 +457,18 @@
     hid = pltpu.VMEM((token_count, columns * block), bf)
     tok_blocks = pltpu.VMEM((tokens.shape[1] // block, token_count, block), bf)
     rows = new_rows.T
+    listed = pltpu.VMEM((nonzero, columns), i32)
     flops = 2 * token_count * slots * block * block
     between = pl.pallas_call(
         functools.partial(kernel, levels, holes, columns, nonzero),
         out_shape=(group, hid, hid, hid, state, state, state, tok_blocks, pltpu.VMEM((3, 8, lanes), i32)),
-        in_specs=[vmem, smem, any_space, any_space, any_space, any_space],
+        in_specs=[any_space] * 8,
         out_specs=(vmem,) * 9,
         scratch_shapes=[
             group, group, group, pltpu.VMEM(tokens.shape, bf), state, state, state, narrow, narrow, halo, halo,
             pltpu.SMEM((4, 8, lanes), i32),
-            pltpu.SemaphoreType.DMA((4,)),
+            listed, listed, listed, pltpu.VMEM((8, lanes), i32), pltpu.SMEM(rows.shape, i32),
+            pltpu.SemaphoreType.DMA((8,)),
             pltpu.SemaphoreType.DMA((4,)),
             pltpu.SemaphoreType.DMA((3,)),
             pltpu.SemaphoreType.DMA((3,)),
@@ -471,19 +483,20 @@
         cost_estimate=pl.CostEstimate(
             flops=3 * flops, bytes_accessed=16 * 1024 * 1024, transcendentals=0
         ),
-    )(pack, rows, tokens, master_old, moment_old, second_old)
+    )(old_cell.T, new_cell.T, regrown.T, rows, tokens, master_old, moment_old, second_old)
     out_state = jax.ShapeDtypeStruct(master_old.shape, f32)
     return pl.pallas_call(
         functools.partial(last_kernel, columns, nonzero),
         out_shape=(
             jax.ShapeDtypeStruct((token_count, ways * columns * block), bf), out_state, out_state, out_state,
         ),
-        in_specs=[vmem] * 9 + [smem],
+        in_specs=[vmem] * 9 + [any_space],
         out_specs=(any_space,) * 4,
         scratch_shapes=[
             hid,
             pltpu.SMEM((8, lanes), i32),
-            pltpu.SemaphoreType.DMA,
+            pltpu.SMEM(rows.shape, i32),
+            pltpu.SemaphoreType.DMA((2,)),
             pltpu.SemaphoreType.DMA((10,)),
         ],
         compiler_params=pltpu.CompilerParams(vmem_limit_bytes=LAST_VMEM),

time: 74.2 us -> 70.7 us (0.953)
  other arithmetic: 1.4 us -> 0 us
  Pallas kernels: 71.3 us -> 69.9 us
    pallas_call x1, Pallas kernels: 67.9 us -> 67.1 us  [on_device_kernel(): pl.pallas_call(functools.partial(kernel, levels, holes, columns, nonzero)...]
where the time goes in v5:
time: 70.7 us; the launch traced here: 70.6 us
  Pallas kernels  69.9 us (99%)
    pallas_call x1, Pallas kernels, on_device_kernel(): pl.pallas_call(functools.partial(kernel, levels, holes, columns, nonzero)...  67.1 us
    pallas_call x1, Pallas kernels, on_device_kernel(): pl.pallas_call(functools.partial(last_kernel, columns, nonzero), out_shap...  2.86 us

profile of v5, /device:TPU:0, one launch (start us, length us, event | category | flops | bytes accessed | tf_op | source)
XLA Modules:
  0.0 70.6 jit_solution(3711804696654662034)
XLA Ops:
  0.6 0.0 copy-start
  0.6 67.1 %shard_map.111 = (bf16[121,128,128]{2,1,0:T(8,128)(2,1)S(1)}, bf16[128,3584]{1,0:T(8,128)(2,1)S(1)}, bf16[128,3584]{1,0:T(8,128)(2,1)S(1)}, bf16[128,3584]{1,0:T...) custom-call(s32[4,28]{1,0:T(4,128)} %bitcast.6, ...), custom_call_target="tpu_custom_call" | custom-call | flops 1409286144 | bytes 16777216 | tf_op jit(solution)/shard_map/pallas_call | solution.py:462
  67.7 0.0 copy-done
  67.7 2.9 %shard_map.112 = (bf16[128,14336]{1,0:T(8,128)(2,1)}, f32[15,128,128]{2,1,0:T(8,128)}, f32[15,128,128]{2,1,0:T(8,128)}, f32[15,128,128]{2,1,0:T(8,128)}) custom-call(bf16[121,128,128]{2,1,0:T(8,128)(2,1)S(1)} %get-tuple-element.13.corner, bf16[128,3584]{1,0:T(8,128)(2,1)S(1)} %get-tuple-element.14.hid0, bf16[128,3584]{1,0:T(8,128)(2,1)S(1)} %get-tuple-element.15.hid1, ...), custom_call_target="tpu_custom_call" | custom-call | flops 469762048 | bytes 8388608 | tf_op jit(solution)/shard_map/pallas_call | solution.py:488
Async XLA Ops:
  0.6 67.1 %copy-start = (s32[112,4]{0,1:T(4,128)S(1)}, s32[112,4]{0,1:T(4,128)}, u32[]{:S(2)}) copy-start(s32[112,4]{0,1:T(4,128)} %param.15) | copy-start | bytes 5380

commit v6 on v5

--- a/solution.py
+++ b/solution.py
@@ -88,7 +88,7 @@
     order = [(r, dz, p) for dz in sorted(others, key=abs) for p in range(PIECES) for r in range(4) if r or dz]
     order.sort(key=lambda k: abs(k[1]) + (k[0] in (1, 2)) + 2 * (k[0] == 3))
     best = None
-    total = 0.66 * 5.2 * capacity
+    total = 0.74 * 5.2 * capacity
     for turn in range(14):
         script = [(0, 0, p) for p in range(PIECES)] + order
         arrived, free = {}, {}
@@ -110,7 +110,7 @@
             place[z] += 1
             for way, there, role_there in onward(levels, z, role, dz, piece):
                 now += 0.15
-                free[z, way] = max(free.get((z, way), 0.0), now) + 0.66 * (cuts[piece + 1] - cuts[piece])
+                free[z, way] = max(free.get((z, way), 0.0), now) + 0.74 * (cuts[piece + 1] - cuts[piece])
                 arrived[there, role_there, z + dz - there, piece] = free[z, way] + 1.0
             clock[z] = now + 0.15
         if turn >= 2 and (best is None or max(clock) < best[0]):
@@ -120,9 +120,9 @@
             came = [arrived[z, key[0], key[1], key[2]] for z in range(levels) if 0 <= z + key[1] < levels]
             held = 0.0
             if key[0] == 3:
-                held = 0.87 if key[2] >= 2 else 0.4
+                held = 0.87 if key[2] >= 2 else 0.55
             elif key[0] and key[2] >= 2:
-                held = 0.68
+                held = 0.6
             mean[key] = max(sum(came) / len(came), held * total)
         order = sorted(order, key=lambda k: (mean[k], k))
     return best[1]
@@ -427,9 +427,9 @@
                 todo += [send_halo, prepare] if role == 0 else []
                 todo += [functools.partial(finish, role)]
                 todo += [functools.partial(compute, role, parts[n], parts[n + 1]) for n in range(4)]
+                todo += [migrate] if last[role] == max(last[r] for r in range(3)) else []
     for act in todo:
         act()
-    migrate()
     finish(3)
 
     for condition, copy in sent:

time: 70.7 us -> 73.9 us (1.045)
  Pallas kernels: 69.9 us -> 73 us
    pallas_call x1, Pallas kernels: 67.1 us -> 70.2 us  [on_device_kernel(): pl.pallas_call(functools.partial(kernel, levels, holes, columns, nonzero)...]
where the time goes in v6:
time: 73.9 us; the launch traced here: 73.7 us
  Pallas kernels  73 us (99%)
    pallas_call x1, Pallas kernels, on_device_kernel(): pl.pallas_call(functools.partial(kernel, levels, holes, columns, nonzero)...  70.2 us
    pallas_call x1, Pallas kernels, on_device_kernel(): pl.pallas_call(functools.partial(last_kernel, columns, nonzero), out_shap...  2.86 us

profile of v6, /device:TPU:0, one launch (start us, length us, event | category | flops | bytes accessed | tf_op | source)
XLA Modules:
  0.0 73.7 jit_solution(8897047354005631562)
XLA Ops:
  0.6 0.0 copy-start
  0.6 70.2 %shard_map.111 = (bf16[121,128,128]{2,1,0:T(8,128)(2,1)S(1)}, bf16[128,3584]{1,0:T(8,128)(2,1)S(1)}, bf16[128,3584]{1,0:T(8,128)(2,1)S(1)}, bf16[128,3584]{1,0:T...) custom-call(s32[4,28]{1,0:T(4,128)} %bitcast.6, ...), custom_call_target="tpu_custom_call" | custom-call | flops 1409286144 | bytes 16777216 | tf_op jit(solution)/shard_map/pallas_call | solution.py:462
  70.8 0.0 copy-done
  70.8 2.9 %shard_map.112 = (bf16[128,14336]{1,0:T(8,128)(2,1)}, f32[15,128,128]{2,1,0:T(8,128)}, f32[15,128,128]{2,1,0:T(8,128)}, f32[15,128,128]{2,1,0:T(8,128)}) custom-call(bf16[121,128,128]{2,1,0:T(8,128)(2,1)S(1)} %get-tuple-element.13.corner, bf16[128,3584]{1,0:T(8,128)(2,1)S(1)} %get-tuple-element.14.hid0, bf16[128,3584]{1,0:T(8,128)(2,1)S(1)} %get-tuple-element.15.hid1, ...), custom_call_target="tpu_custom_call" | custom-call | flops 469762048 | bytes 8388608 | tf_op jit(solution)/shard_map/pallas_call | solution.py:488
Async XLA Ops:
  0.6 70.2 %copy-start = (s32[112,4]{0,1:T(4,128)S(1)}, s32[112,4]{0,1:T(4,128)}, u32[]{:S(2)}) copy-start(s32[112,4]{0,1:T(4,128)} %param.15) | copy-start | bytes 5380
